TPU v7x, 32 devices: a whole 2x2x4 slice. The times are simulated.
32 devices in a mesh: group: 2 (over x), dx: 16 (over z, y, core).
Axes of the slice: x: 2, y: 2, z: 4, core: 2. Of those that a mesh axis runs over, the one named last changes fastest.
Arguments:
- points: bfloat16 [16384, 1024], P(('group', 'dx')), parts along dimension 0, may hold values from -6 to 6
- cotangent: bfloat16 [16384, 1024], P(('group', 'dx')), parts along dimension 0, may hold values from -96 to 96
- counts: int32 [32], P(('group', 'dx')), parts along dimension 0, may hold values from 170 to 512, as said below
- w_query: bfloat16 [1024, 1024], replicated, may hold values from -0.1875 to 0.1875
- w_key: bfloat16 [1024, 1024], replicated, may hold values from -0.1875 to 0.1875
- w_value: bfloat16 [1024, 1024], replicated, may hold values from -0.1875 to 0.1875
- gain_key: float32 [1024], replicated, may hold values from 0.25 to 1.75
- bias_key: float32 [1024], replicated, may hold values from -3 to 3
- gain_value: float32 [1024], replicated, may hold values from 0.25 to 1.75
- bias_value: float32 [1024], replicated, may hold values from -3 to 3
Outputs:
- grad_points: bfloat16 [16384, 1024], P(('group', 'dx')), parts along dimension 0
There are 2 independent parts, one for each index of `group`. A program takes and returns all parts, laid end to end along the dimension named above; an argument that names none is the same for every part. Nothing has to cross between parts.
Inputs may be any that keep to these rules, and one draw needn't show every extreme that they name: `counts`: live points of each tile; some tile of every slab holds 512.
All inputs are finite; a program needn't handle non-finite values.
Results may differ from a plain program's by a relative error of at most 0.006.
Values sent between devices are 32-bit elements; how exact they have to be, the bound alone decides.
A program may use at most 64 MiB of HBM per device.

v0:
```python
import jax
import jax.numpy as jnp
from jax import lax
from jax.sharding import PartitionSpec as P

HEADS = 8
eps = 1e-05


def head_norm(raw, heads):
    grouped = raw.reshape(raw.shape[0], heads, -1)
    center = grouped - jnp.mean(grouped, axis=2, keepdims=True)
    inverse = lax.rsqrt(jnp.mean(center * center, axis=2, keepdims=True) + eps)
    return (center * inverse, inverse)


def norm_back(grad, gain, normed, inverse, heads):
    scaled = grad * gain.reshape(heads, -1)
    inner = scaled - jnp.mean(scaled, axis=2, keepdims=True)
    inner = inner - normed * jnp.mean(scaled * normed, axis=2, keepdims=True)
    return (inverse * inner).reshape(grad.shape[0], -1).astype(jnp.bfloat16)


def body(
    points, cotangent, counts, w_query, w_key, w_value, gain_key, bias_key, gain_value, bias_value
):
    rows = points.shape[0]
    heads = HEADS
    live = (lax.iota(jnp.int32, rows) < counts[0]).astype(jnp.float32)[:, None]
    live_h = live[:, :, None]
    own_count = counts[0].astype(jnp.float32)
    total = lax.psum(own_count, "dx")
    key_hat, key_inv = head_norm(jnp.dot(points, w_key, preferred_element_type=jnp.float32), heads)
    value_hat, value_inv = head_norm(
        jnp.dot(points, w_value, preferred_element_type=jnp.float32), heads
    )
    keys = (live_h * (key_hat * gain_key.reshape(heads, -1) + bias_key.reshape(heads, -1))).astype(
        jnp.bfloat16
    )
    values = (
        live_h * (value_hat * gain_value.reshape(heads, -1) + bias_value.reshape(heads, -1))
    ).astype(jnp.bfloat16)
    kv_local = jnp.einsum("nhi,nhj->hij", keys, values, preferred_element_type=jnp.float32)
    cot = cotangent.reshape(rows, heads, -1)
    kv_sum = lax.psum(kv_local, "dx")
    query = jnp.dot(points, w_query, preferred_element_type=jnp.float32).astype(jnp.bfloat16)
    masked_query = (query * live.astype(jnp.bfloat16)).reshape(rows, heads, -1)
    qdy_local = jnp.einsum("nhi,nhj->hij", masked_query, cot, preferred_element_type=jnp.float32)
    qdy_sum = lax.psum(qdy_local, "dx")
    gram = (kv_sum / total).astype(jnp.bfloat16)
    dgram = (qdy_sum / total).astype(jnp.bfloat16)
    dquery = (
        (live_h * jnp.einsum("nhj,hij->nhi", cot, gram, preferred_element_type=jnp.float32))
        .reshape(rows, -1)
        .astype(jnp.bfloat16)
    )
    dkeys = jnp.einsum("nhj,hij->nhi", values, dgram, preferred_element_type=jnp.float32)
    dvalues = jnp.einsum("nhi,hij->nhj", keys, dgram, preferred_element_type=jnp.float32)
    dkey_raw = norm_back(dkeys, gain_key, key_hat, key_inv, heads)
    dvalue_raw = norm_back(dvalues, gain_value, value_hat, value_inv, heads)
    grad = jnp.dot(dquery, w_query.T, preferred_element_type=jnp.float32)
    grad = grad + jnp.dot(dkey_raw, w_key.T, preferred_element_type=jnp.float32)
    grad = grad + jnp.dot(dvalue_raw, w_value.T, preferred_element_type=jnp.float32)
    return grad.astype(jnp.bfloat16)


def solution(mesh):
    placed = (
        P(("group", "dx"), None),
        P(("group", "dx"), None),
        P(("group", "dx")),
        P(),
        P(),
        P(),
        P(),
        P(),
        P(),
        P(),
    )
    return jax.shard_map(
        body, mesh=mesh, in_specs=placed, out_specs=P(("group", "dx"), None), check_vma=False
    )
```

profile of v0, /device:TPU:0, one launch (start us, length us, event | category | flops | bytes accessed | tf_op | source)
XLA Modules:
  0.0 156.2 jit_solution(9435731812244880489)
XLA Ops:
  6.5 3.3 %convolution_bitcast_fusion = f32[64,8,8,128]{3,1,2,0:T(8,128)S(1)} fusion(bf16[512,1024]{1,0:T(8,128)(2,1)} %param.10, bf16[1024,1024]{1,0:T(8,128)(2,1)} %param.15), kind=kOutput, calls=%fused_computation.22 | convolution fusion | flops 1073741824 | bytes 5242880 | tf_op jit(solution)/shard_map/dot_general | solution.py:35
  9.8 1.8 %copy.72 = f32[64,8,8,128]{3,2,1,0:T(8,128)} copy(f32[64,8,8,128]{3,1,2,0:T(8,128)S(1)} %convolution_bitcast_fusion) | data formatting | bytes 4194304
  11.6 3.0 %copy.57 = f32[512,8,128]{0,2,1:T(8,128)} copy(f32[512,8,128]{2,1,0:T(8,128)} %bitcast.70) | data formatting | bytes 4194304 | tf_op jit(solution)/shard_map/reshape | solution.py:11
  14.6 2.3 %reduce_sum.74 = f32[512,8]{1,0:T(8,128)S(1)} reduce(f32[512,8,128]{2,1,0:T(8,128)} %bitcast.71, f32[]{:T(128)} %constant.11.clone.1), dimensions={2}, to_apply=%region_2.0 | reduce | flops 520192 | bytes 2113540 | tf_op jit(solution)/shard_map/reduce_sum | solution.py:12
  16.9 1.3 convolution_bitcast_fusion.1
  18.2 1.8 %copy.71 = f32[64,8,8,128]{3,2,1,0:T(8,128)} copy(f32[64,8,8,128]{3,1,2,0:T(8,128)S(1)} %convolution_bitcast_fusion.1) | data formatting | bytes 4194304
  20.0 2.9 %copy.55 = f32[512,8,128]{0,2,1:T(8,128)} copy(f32[512,8,128]{2,1,0:T(8,128)} %bitcast.68) | data formatting | bytes 4194304 | tf_op jit(solution)/shard_map/reshape | solution.py:11
  22.9 2.2 %reduce_sum.72 = f32[512,8]{1,0:T(8,128)S(1)} reduce(f32[512,8,128]{2,1,0:T(8,128)} %bitcast.69, f32[]{:T(128)} %constant.11.clone.1), dimensions={2}, to_apply=%region_0.0 | reduce | flops 520192 | bytes 2113540 | tf_op jit(solution)/shard_map/reduce_sum | solution.py:12
  25.1 0.1 copy.56
  25.2 0.1 copy.54
  26.0 4.1 %fusion.8 = bf16[512,1024]{1,0:T(8,128)(2,1)} fusion(bf16[512,1024]{1,0:T(8,128)(2,1)} %param.10, bf16[1024,1024]{1,0:T(8,128)(2,1)} %param.13, bf16[512]{0:T(512)(128)(2,1)S(1)} %get-tuple-element.14), kind=kOutput, calls=%fused_computation.25 | convolution fusion | flops 1074790400 | bytes 4195328 | tf_op jit(solution)/shard_map/dot_general | solution.py:46
  30.2 1.5 copy.69
  31.7 0.0 copy-start.5
  31.7 2.0 %multiply_reduce_fusion = f32[512,8]{0,1:T(8,128)S(1)} fusion(f32[512,8,128]{0,2,1:T(8,128)} %copy.57, f32[512,8]{0,1:T(8,128)S(1)} %broadcast_multiply_fusion.4), kind=kLoop, calls=%fused_computation.17 | loop fusion | flops 1568768 | bytes 2129920 | tf_op jit(solution)/shard_map/reduce_sum | solution.py:13
  33.7 0.2 copy-done.3
  33.9 0.3 multiply_reduce_fusion.1
  34.2 1.3 fusion.9
  35.5 0.0 copy-done.1
  35.6 2.0 %fusion.18 = f32[8,128,128]{2,1,0:T(8,128)} fusion(f32[512,8,128]{0,2,1:T(8,128)S(1)} %copy-done.3, f32[8,128]{1,0:T(8,128)S(1)} %bitcast.83, f32[8,128]{1,0:T(8,128)S(1)} %bitcast.75, f32[512,8]{0,1:T(8,128)S(1)} %get-tuple-element.16, f32[512,8]{0,1:T(8,128)S(1)} %broadcast_multiply_fusion.5, f32[512]{0:T(512)S(1)} %get-tuple-element.13, ...), kind=kOutput, calls=%fused_computation.46 | convolution fusion | flops 140509184 | bytes 4802560 | tf_op jit(solution)/shard_map/nhi,nhj->hij/dot_general | solution.py:43
  37.5 0.0 all-reduce.3.cloned.1.call-update
  37.6 35.9 %psum.22 = f32[]{:T(128)} all-reduce(f32[]{:T(128)S(6)} %convert_element_type.64), channel_id=1, replica_groups=mesh['group'=2,'dx'=16] {'dx'}, use_global_device_ids=true, to_apply=%region_5.0 | all-reduce | flops 1 | bytes 8 | tf_op jit(solution)/shard_map/psum | solution.py:32
  73.5 60.4 %all-reduce.3.cloned.1.call-done = (f32[8,128,128]{2,1,0:T(8,128)}, f32[8,128,128]{2,1,0:T(8,128)}) async-done(((f32[8,128,128]{2,1,0:T(8,128)}, f32[8,128,128]{2,1,0:T(8,128)}), (f32[8,128,128]{2,1,0:T(8,128)}, f32[8,128,128]{2,1,0:T(8,128)})) %all-reduce.3.cloned.1.call-update) | async-done | bytes 1048592 | tf_op jit(solution)/shard_map/psum | solution.py:45
  133.9 4.8 %bitcast_reduce_fusion = (f32[512,8]{0,1:T(8,128)S(1)}, f32[512,8]{0,1:T(8,128)S(1)}, f32[8,128,512]{2,1,0:T(8,128)S(1)}) fusion(f32[8,128]{1,0:T(8,128)S(1)} %bitcast.80, f32[512,8]{0,1:T(8,128)S(1)} %get-tuple-element.15, f32[512,8,128]{0,2,1:T(8,128)} %copy.57, f32[512,8]{0,1:T(8,128)S(1)} %broadcast_multiply_fusion.4, f32[512,8,128]{0,2,1:T(8,128)} %copy.55, ...), kind=kOutput, calls=%fused_computation.2 | convolution fusion | flops 140763136 | bytes 6928388 | tf_op jit(solution)/shard_map/nhi,hij->nhj/dot_general | solution.py:58
  138.7 1.7 %bitcast_reduce_fusion.1 = (f32[512,8]{0,1:T(8,128)S(1)}, f32[512,8]{0,1:T(8,128)S(1)}, f32[8,128,512]{2,1,0:T(8,128)S(1)}) fusion(f32[8,128]{1,0:T(8,128)S(1)} %bitcast.77, f32[512,8]{0,1:T(8,128)S(1)} %get-tuple-element.16, f32[512,8,128]{0,2,1:T(8,128)S(1)} %copy-done.4, f32[512,8]{0,1:T(8,128)S(1)} %broadcast_multiply_fusion.5, ...), kind=kOutput, calls=%fused_computation.9 | convolution fusion | flops 140763136 | bytes 6928388 | tf_op jit(solution)/shard_map/nhj,hij->nhi/dot_general | solution.py:57
  140.5 0.8 fusion.6
  141.3 1.3 fusion.21
  142.6 1.3 multiply_convert_fusion
  143.9 0.3 copy-done.9
  144.2 1.3 fusion.20
  145.5 0.8 fusion.2
  146.3 0.8 copy-done.10
  147.1 2.3 %add_convert_fusion = bf16[512,1024]{1,0:T(8,128)(2,1)} fusion(f32[512,1024]{1,0:T(8,128)S(1)} %fusion.20, f32[512,1024]{1,0:T(8,128)S(1)} %fusion.21, bf16[512,1024]{0,1:T(8,128)(2,1)S(1)} %bitcast.73, bf16[1024,1024]{1,0:T(8,128)(2,1)S(1)} %copy-done.10), kind=kOutput, calls=%fused_computation.14 | convolution fusion | flops 1075314688 | bytes 8388608 | tf_op jit(solution)/shard_map/dot_general | solution.py:63
  (36 shorter events, 0.1 us)
Async XLA Ops:
  6.5 10.4 %copy-start = (bf16[1024,1024]{1,0:T(8,128)(2,1)S(1)}, bf16[1024,1024]{1,0:T(8,128)(2,1)}, u32[]{:S(2)}) copy-start(bf16[1024,1024]{1,0:T(8,128)(2,1)} %param.14) | copy-start | bytes 6291460
  6.5 127.3 %all-reduce.3.cloned.1.call-start = ((), (), s32[]{:S(2)}) async-start(), calls=%async_computation | async-start | bytes 2097152 | tf_op jit(solution)/shard_map/psum | solution.py:45
  14.6 2.3 %copy-start.11 = (bf16[512,1024]{1,0:T(8,128)(2,1)S(1)}, bf16[512,1024]{1,0:T(8,128)(2,1)}, u32[]{:S(2)}) copy-start(bf16[512,1024]{1,0:T(8,128)(2,1)} %param.10) | copy-start | bytes 3145732
  31.7 2.2 %copy-start.3 = (f32[512,8,128]{0,2,1:T(8,128)S(1)}, f32[512,8,128]{0,2,1:T(8,128)}, u32[]{:S(2)}) copy-start(f32[512,8,128]{0,2,1:T(8,128)} %copy.55) | copy-start | bytes 6291460
  31.7 2.6 %copy-start.5 = (bf16[512,1024]{1,0:T(8,128)(2,1)S(1)}, bf16[512,1024]{1,0:T(8,128)(2,1)}, u32[]{:S(2)}) copy-start(bf16[512,1024]{1,0:T(8,128)(2,1)} %param.11) | copy-start | bytes 3145732
  33.9 1.7 %copy-start.1 = (f32[512,8,128]{0,2,1:T(8,128)S(1)}, f32[512,8,128]{0,2,1:T(8,128)}, u32[]{:S(2)}) copy-start(f32[512,8,128]{0,2,1:T(8,128)} %copy.57) | copy-start | bytes 6291460
  33.9 1.7 %copy-start.7 = (f32[1024]{0:T(1024)S(1)}, f32[1024]{0:T(1024)}, u32[]{:S(2)}) copy-start(f32[1024]{0:T(1024)} %param.16) | copy-start | bytes 12292
  33.9 1.7 %copy-start.8 = (f32[1024]{0:T(1024)S(1)}, f32[1024]{0:T(1024)}, u32[]{:S(2)}) copy-start(f32[1024]{0:T(1024)} %param.18) | copy-start | bytes 12292
  33.9 1.7 %copy-start.14 = (f32[1024]{0:T(1024)S(1)}, f32[1024]{0:T(1024)}, u32[]{:S(2)}) copy-start(f32[1024]{0:T(1024)} %param.17) | copy-start | bytes 12292
  33.9 1.7 %copy-start.15 = (f32[1024]{0:T(1024)S(1)}, f32[1024]{0:T(1024)}, u32[]{:S(2)}) copy-start(f32[1024]{0:T(1024)} %param.19) | copy-start | bytes 12292
  133.9 4.8 %copy-start.2 = (f32[512,8,128]{0,2,1:T(8,128)S(1)}, f32[512,8,128]{0,2,1:T(8,128)}, u32[]{:S(2)}) copy-start(f32[512,8,128]{0,2,1:T(8,128)} %copy.57) | copy-start | bytes 6291460
  133.9 4.8 %copy-start.4 = (f32[512,8,128]{0,2,1:T(8,128)S(1)}, f32[512,8,128]{0,2,1:T(8,128)}, u32[]{:S(2)}) copy-start(f32[512,8,128]{0,2,1:T(8,128)} %copy.55) | copy-start | bytes 6291460
  133.9 4.8 %copy-start.13 = (f32[8,128,128]{2,1,0:T(8,128)S(1)}, f32[8,128,128]{2,1,0:T(8,128)}, u32[]{:S(2)}) copy-start(f32[8,128,128]{2,1,0:T(8,128)} %get-tuple-element.10) | copy-start | bytes 1572868
  141.3 1.4 copy-start.6
  141.3 1.4 copy-start.12
  142.6 1.6 %copy-start.9 = (bf16[1024,1024]{1,0:T(8,128)(2,1)S(1)}, bf16[1024,1024]{1,0:T(8,128)(2,1)}, u32[]{:S(2)}) copy-start(bf16[1024,1024]{1,0:T(8,128)(2,1)} %param.13) | copy-start | bytes 6291460
  145.5 1.6 %copy-start.10 = (bf16[1024,1024]{1,0:T(8,128)(2,1)S(1)}, bf16[1024,1024]{1,0:T(8,128)(2,1)}, u32[]{:S(2)}) copy-start(bf16[1024,1024]{1,0:T(8,128)(2,1)} %param.15) | copy-start | bytes 6291460
Sparse Core Ops, SparseCore 0:
  37.7 96.1 all-reduce.2
where the time goes:
time: 157 us; the launch traced here: 156 us
  waiting for transfers between devices  60.4 us (38%)
  blocking collectives  35.9 us (23%)
  matrix products  24.6 us (16%)
  between operations  14.3 us (9%)
  local copies, waits for them, and re-layouts  12.5 us (8%)
  other arithmetic  8.47 us (5%)
    psum x1, waiting for transfers between devices, body(): kv_sum = lax.psum(kv_local, 'dx')  60.4 us
    psum x1, blocking collectives, body(): total = lax.psum(own_count, 'dx')  35.9 us
    reshape x2, local copies, waits for them, and re-layouts, head_norm(): grouped = raw.reshape(raw.shape[0], heads, -1)  5.92 us
    unnamed x34, local copies, waits for them, and re-layouts  4.87 us
    dot_general x1, matrix products, body(): jnp.einsum('nhi,hij->nhj', keys, dgram, preferred_element_type=jnp.float32)  4.81 us
    reduce_sum x2, other arithmetic, head_norm(): center = grouped - jnp.mean(grouped, axis=2, keepdims=True)  4.51 us
    dot_general x1, matrix products, body(): jnp.dot(points, w_query, preferred_element_type=jnp.float32)  4.15 us
    dot_general x1, matrix products, body(): jnp.dot(points, w_value, preferred_element_type=jnp.float32)  3.3 us
  transfers between devices with their start and end apart: 1, of which 1 were waited for; matrix products, arithmetic and copies ran while one was open for 0% of the time, Pallas kernels for 0%

commit v1 on v0

--- a/solution.py
+++ b/solution.py
@@ -2,6 +2,7 @@
 import jax.numpy as jnp
 from jax import lax
 from jax.sharding import PartitionSpec as P
+from jax.lax import all_gather
 
 HEADS = 8
 eps = 1e-05
@@ -42,7 +43,7 @@
     ).astype(jnp.bfloat16)
     kv_local = jnp.einsum("nhi,nhj->hij", keys, values, preferred_element_type=jnp.float32)
     cot = cotangent.reshape(rows, heads, -1)
-    kv_sum = lax.psum(kv_local, "dx")
+    kv_sum = all_gather(kv_local, axis_name="dx").sum(axis=0)
     query = jnp.dot(points, w_query, preferred_element_type=jnp.float32).astype(jnp.bfloat16)
     masked_query = (query * live.astype(jnp.bfloat16)).reshape(rows, heads, -1)
     qdy_local = jnp.einsum("nhi,nhj->hij", masked_query, cot, preferred_element_type=jnp.float32)

time: 157 us -> 205 us (1.31)
  waiting for transfers between devices: 60.4 us -> 99.6 us
  other arithmetic: 8.47 us -> 14.3 us
  matrix products: 24.6 us -> 27.7 us
    all_gather x0 -> x1, waiting for transfers between devices: none -> 66 us  [body(): kv_sum = all_gather(kv_local, axis_name='dx').sum(axis=0)]
    psum x1, waiting for transfers between devices: 60.4 us -> 33.6 us  [body(): qdy_sum = lax.psum(qdy_local, 'dx')]
    reduce_sum x0 -> x1, other arithmetic: none -> 4.85 us  [body(): kv_sum = all_gather(kv_local, axis_name='dx').sum(axis=0)]
  transfers between devices with their start and end apart: 1 -> 2, of which waited for: 1 -> 2; matrix products, arithmetic and copies ran while one was open for 0% -> 17% of each run, Pallas kernels for 0% -> 0%
where the time goes in v1:
time: 205 us
  waiting for transfers between devices  99.6 us (49%)
  blocking collectives  35.8 us (17%)
  matrix products  27.7 us (14%)
  between operations  14.5 us (7%)
  other arithmetic  14.3 us (7%)
  local copies, waits for them, and re-layouts  12.9 us (6%)
    all_gather x1, waiting for transfers between devices, body(): kv_sum = all_gather(kv_local, axis_name='dx').sum(axis=0)  66 us
    psum x1, blocking collectives, body(): total = lax.psum(own_count, 'dx')  35.8 us
    psum x1, waiting for transfers between devices, body(): qdy_sum = lax.psum(qdy_local, 'dx')  33.6 us
    reshape x2, local copies, waits for them, and re-layouts, head_norm(): grouped = raw.reshape(raw.shape[0], heads, -1)  5.86 us
    unnamed x34, local copies, waits for them, and re-layouts  5.33 us
    reduce_sum x1, other arithmetic, body(): kv_sum = all_gather(kv_local, axis_name='dx').sum(axis=0)  4.85 us
    dot_general x1, matrix products, body(): jnp.einsum('nhi,hij->nhj', keys, dgram, preferred_element_type=jnp.float32)  4.64 us
    reduce_sum x2, other arithmetic, head_norm(): center = grouped - jnp.mean(grouped, axis=2, keepdims=True)  4.53 us
  transfers between devices with their start and end apart: 2, of which 2 were waited for; matrix products, arithmetic and copies ran while one was open for 17% of the time, Pallas kernels for 0%

profile of v1, /device:TPU:0, one launch (start us, length us, event | category | flops | bytes accessed | tf_op | source)
XLA Modules:
  0.0 204.9 jit_solution(13449697773431012890)
XLA Ops:
  7.4 4.1 %fusion.8 = bf16[512,1024]{1,0:T(8,128)(2,1)} fusion(bf16[512,1024]{1,0:T(8,128)(2,1)} %param.10, bf16[1024,1024]{1,0:T(8,128)(2,1)} %param.13, bf16[512]{0:T(512)(128)(2,1)S(1)} %fusion.16), kind=kOutput, calls=%fused_computation.25 | convolution fusion | flops 1074790400 | bytes 4195328 | tf_op jit(solution)/shard_map/dot_general | solution.py:47
  11.5 1.5 copy.71
  13.0 2.5 %fusion.9 = f32[8,128,128]{2,1,0:T(8,128)} fusion(bf16[512,8,128]{0,2,1:T(8,128)(2,1)S(1)} %bitcast.75, bf16[512,1024]{1,0:T(8,128)(2,1)} %param.11), kind=kOutput, calls=%fused_computation.26 | convolution fusion | flops 134217728 | bytes 2621440 | tf_op jit(solution)/shard_map/nhi,nhj->hij/dot_general | solution.py:49
  15.6 3.2 %convolution_bitcast_fusion = f32[64,8,8,128]{3,1,2,0:T(8,128)S(1)} fusion(bf16[512,1024]{1,0:T(8,128)(2,1)} %param.10, bf16[1024,1024]{1,0:T(8,128)(2,1)} %param.15), kind=kOutput, calls=%fused_computation.22 | convolution fusion | flops 1073741824 | bytes 5242880 | tf_op jit(solution)/shard_map/dot_general | solution.py:36
  18.7 1.8 copy.74
  20.5 3.0 %copy.59 = f32[512,8,128]{0,2,1:T(8,128)} copy(f32[512,8,128]{2,1,0:T(8,128)} %bitcast.70) | data formatting | bytes 4194304 | tf_op jit(solution)/shard_map/reshape | solution.py:12
  23.5 2.3 %reduce_sum.83 = f32[512,8]{1,0:T(8,128)S(1)} reduce(f32[512,8,128]{2,1,0:T(8,128)} %bitcast.71, f32[]{:T(128)} %constant.11.clone.1), dimensions={2}, to_apply=%region_2.0 | reduce | flops 520192 | bytes 2113540 | tf_op jit(solution)/shard_map/reduce_sum | solution.py:13
  25.8 1.3 convolution_bitcast_fusion.1
  27.1 1.8 copy.73
  28.9 2.9 %copy.57 = f32[512,8,128]{0,2,1:T(8,128)} copy(f32[512,8,128]{2,1,0:T(8,128)} %bitcast.72) | data formatting | bytes 4194304 | tf_op jit(solution)/shard_map/reshape | solution.py:12
  31.8 2.2 %reduce_sum.81 = f32[512,8]{1,0:T(8,128)S(1)} reduce(f32[512,8,128]{2,1,0:T(8,128)} %bitcast.73, f32[]{:T(128)} %constant.11.clone.1), dimensions={2}, to_apply=%region_0.0 | reduce | flops 520192 | bytes 2113540 | tf_op jit(solution)/shard_map/reduce_sum | solution.py:13
  34.0 0.1 copy.58
  34.1 0.1 copy.56
  34.3 2.1 %multiply_reduce_fusion = f32[512,8]{0,1:T(8,128)S(1)} fusion(f32[512,8,128]{0,2,1:T(8,128)} %copy.59, f32[512,8]{0,1:T(8,128)S(1)} %broadcast_multiply_fusion.4), kind=kLoop, calls=%fused_computation.17 | loop fusion | flops 1568768 | bytes 2129920 | tf_op jit(solution)/shard_map/reduce_sum | solution.py:14
  36.4 0.1 copy-done.1
  36.5 0.3 multiply_reduce_fusion.1
  36.8 0.3 copy-done.3
  37.1 2.0 fusion.18
  39.2 35.8 %psum.14 = f32[]{:T(128)} all-reduce(f32[]{:T(128)S(6)} %convert_element_type.64), channel_id=1, replica_groups=mesh['group'=2,'dx'=16] {'dx'}, use_global_device_ids=true, to_apply=%region_5.0 | all-reduce | flops 1 | bytes 8 | tf_op jit(solution)/shard_map/psum | solution.py:33
  75.0 33.6 %all-reduce.2.cloned.1.call-done = f32[8,128,128]{2,1,0:T(8,128)} async-done(((f32[8,128,128]{2,1,0:T(8,128)}), f32[8,128,128]{2,1,0:T(8,128)}) %all-reduce.2.cloned.1.call-update) | async-done | bytes 524304 | tf_op jit(solution)/shard_map/psum | solution.py:50
  108.5 4.6 %bitcast_reduce_fusion = (f32[512,8]{0,1:T(8,128)S(1)}, f32[512,8]{0,1:T(8,128)S(1)}, f32[8,128,512]{2,1,0:T(8,128)S(1)}) fusion(f32[8,128]{1,0:T(8,128)S(1)} %bitcast.79, f32[512,8]{0,1:T(8,128)S(1)} %get-tuple-element.11, f32[512,8,128]{0,2,1:T(8,128)} %copy.59, f32[512,8]{0,1:T(8,128)S(1)} %broadcast_multiply_fusion.4, f32[512,8,128]{0,2,1:T(8,128)} %copy.57, ...), kind=kOutput, calls=%fused_computation.2 | convolution fusion | flops 140763136 | bytes 6928388 | tf_op jit(solution)/shard_map/nhi,hij->nhj/dot_general | solution.py:59
  113.2 1.6 bitcast_reduce_fusion.1
  114.8 1.8 fusion.2
  116.6 0.8 fusion.6
  117.4 2.7 %fusion.21 = f32[512,1024]{1,0:T(8,128)} fusion(bf16[512,1024]{0,1:T(8,128)(2,1)S(1)} %bitcast.77, bf16[1024,1024]{1,0:T(8,128)(2,1)S(1)} %copy-done), kind=kOutput, calls=%fused_computation.49 | convolution fusion | flops 1073741824 | bytes 5242880 | tf_op jit(solution)/shard_map/dot_general | solution.py:63
  120.1 66.0 %all-gather.3.cloned.1.call-done = f32[128,128,128]{2,1,0:T(8,128)} async-done(((f32[8,128,128]{2,1,0:T(8,128)}), f32[128,128,128]{2,1,0:T(8,128)}) %all-gather.3.cloned.1.call-update) | async-done | bytes 8388624 | tf_op jit(solution)/shard_map/all_gather | solution.py:46
  186.1 4.8 %reduce_sum.85 = f32[8,128,128]{2,1,0:T(8,128)} reduce(f32[16,8,128,128]{3,2,1,0:T(8,128)} %bitcast.74, f32[]{:T(128)} %constant.11.clone.1), dimensions={0}, to_apply=%region_4.0 | reduce | flops 1966080 | bytes 8912900 | tf_op jit(solution)/shard_map/reduce_sum | solution.py:46
  191.0 2.2 %multiply_convert_fusion = bf16[8,128,512]{2,1,0:T(8,128)(2,1)S(1)} fusion(f32[512]{0:T(512)S(1)} %fusion.15, f32[8,128,128]{2,1,0:T(8,128)} %reduce_sum.85, f32[]{:T(128)} %psum.14, bf16[512,1024]{1,0:T(8,128)(2,1)S(1)} %copy-done.5), kind=kOutput, calls=%fused_computation.15 | convolution fusion | flops 135528448 | bytes 2623492 | tf_op jit(solution)/shard_map/nhj,hij->nhi/dot_general | solution.py:54
  193.2 1.3 fusion.20
  194.5 0.6 copy-done.10
  195.1 0.6 copy-done.15
  195.8 2.3 %add_convert_fusion = bf16[512,1024]{1,0:T(8,128)(2,1)} fusion(f32[512,1024]{1,0:T(8,128)S(1)} %fusion.20, f32[512,1024]{1,0:T(8,128)S(1)} %copy-done.15, bf16[512,1024]{0,1:T(8,128)(2,1)S(1)} %bitcast.76, bf16[1024,1024]{1,0:T(8,128)(2,1)S(1)} %copy-done.10), kind=kOutput, calls=%fused_computation.14 | convolution fusion | flops 1075314688 | bytes 8388608 | tf_op jit(solution)/shard_map/dot_general | solution.py:64
  (41 shorter events, 0.2 us)
Async XLA Ops:
  6.5 19.3 %copy-start = (bf16[1024,1024]{1,0:T(8,128)(2,1)S(1)}, bf16[1024,1024]{1,0:T(8,128)(2,1)}, u32[]{:S(2)}) copy-start(bf16[1024,1024]{1,0:T(8,128)(2,1)} %param.14) | copy-start | bytes 6291460
  6.5 102.0 %all-reduce.2.cloned.1.call-start = ((), (), s32[]{:S(2)}) async-start(), calls=%async_computation | async-start | bytes 1048576 | tf_op jit(solution)/shard_map/psum | solution.py:50
  15.5 170.6 %all-gather.3.cloned.1.call-start = ((), (), s32[]{:S(2)}) async-start(), calls=%async_computation.1 | async-start | bytes 8912896 | tf_op jit(solution)/shard_map/all_gather | solution.py:46
  23.5 2.3 %copy-start.11 = (bf16[512,1024]{1,0:T(8,128)(2,1)S(1)}, bf16[512,1024]{1,0:T(8,128)(2,1)}, u32[]{:S(2)}) copy-start(bf16[512,1024]{1,0:T(8,128)(2,1)} %param.10) | copy-start | bytes 3145732
  34.2 2.3 %copy-start.1 = (f32[512,8,128]{0,2,1:T(8,128)S(1)}, f32[512,8,128]{0,2,1:T(8,128)}, u32[]{:S(2)}) copy-start(f32[512,8,128]{0,2,1:T(8,128)} %copy.57) | copy-start | bytes 6291460
  34.3 2.9 %copy-start.3 = (f32[512,8,128]{0,2,1:T(8,128)S(1)}, f32[512,8,128]{0,2,1:T(8,128)}, u32[]{:S(2)}) copy-start(f32[512,8,128]{0,2,1:T(8,128)} %copy.59) | copy-start | bytes 6291460
  34.3 2.9 %copy-start.7 = (f32[1024]{0:T(1024)S(1)}, f32[1024]{0:T(1024)}, u32[]{:S(2)}) copy-start(f32[1024]{0:T(1024)} %param.18) | copy-start | bytes 12292
  34.3 2.8 %copy-start.8 = (f32[1024]{0:T(1024)S(1)}, f32[1024]{0:T(1024)}, u32[]{:S(2)}) copy-start(f32[1024]{0:T(1024)} %param.16) | copy-start | bytes 12292
  34.3 2.8 %copy-start.13 = (f32[1024]{0:T(1024)S(1)}, f32[1024]{0:T(1024)}, u32[]{:S(2)}) copy-start(f32[1024]{0:T(1024)} %param.17) | copy-start | bytes 12292
  34.3 2.8 %copy-start.14 = (f32[1024]{0:T(1024)S(1)}, f32[1024]{0:T(1024)}, u32[]{:S(2)}) copy-start(f32[1024]{0:T(1024)} %param.19) | copy-start | bytes 12292
  108.5 4.7 %copy-start.2 = (f32[512,8,128]{0,2,1:T(8,128)S(1)}, f32[512,8,128]{0,2,1:T(8,128)}, u32[]{:S(2)}) copy-start(f32[512,8,128]{0,2,1:T(8,128)} %copy.57) | copy-start | bytes 6291460
  108.5 4.7 %copy-start.4 = (f32[512,8,128]{0,2,1:T(8,128)S(1)}, f32[512,8,128]{0,2,1:T(8,128)}, u32[]{:S(2)}) copy-start(f32[512,8,128]{0,2,1:T(8,128)} %copy.59) | copy-start | bytes 6291460
  108.5 4.7 %copy-start.12 = (f32[8,128,128]{2,1,0:T(8,128)S(1)}, f32[8,128,128]{2,1,0:T(8,128)}, u32[]{:S(2)}) copy-start(f32[8,128,128]{2,1,0:T(8,128)} %all-reduce.2.cloned.1.call-done) | copy-start | bytes 1572868
  186.1 4.9 %copy-start.5 = (bf16[512,1024]{1,0:T(8,128)(2,1)S(1)}, bf16[512,1024]{1,0:T(8,128)(2,1)}, u32[]{:S(2)}) copy-start(bf16[512,1024]{1,0:T(8,128)(2,1)} %param.11) | copy-start | bytes 3145732
  191.0 2.2 %copy-start.9 = (bf16[1024,1024]{1,0:T(8,128)(2,1)S(1)}, bf16[1024,1024]{1,0:T(8,128)(2,1)}, u32[]{:S(2)}) copy-start(bf16[1024,1024]{1,0:T(8,128)(2,1)} %param.13) | copy-start | bytes 6291460
  193.2 1.3 copy-start.6
  193.2 1.9 copy-start.10
  193.2 2.5 %copy-start.15 = (f32[512,1024]{1,0:T(8,128)S(1)}, f32[512,1024]{1,0:T(8,128)}, u32[]{:S(2)}) copy-start(f32[512,1024]{1,0:T(8,128)} %fusion.21) | copy-start | bytes 6291460
Sparse Core Ops, SparseCore 0:
  15.6 92.8 all-reduce.1
  110.7 75.3 all-gather.2
